TPU v7x, 32 devices: a whole 2x2x4 slice. The times are simulated.
32 devices in a mesh: ctx: 8 (over y, x, core), kv: 4 (over z).
Axes of the slice: x: 2, y: 2, z: 4, core: 2. Of those that a mesh axis runs over, the one named last changes fastest.
Arguments:
- queries: bfloat16 [4096, 32, 128], P('ctx', 'kv'), may hold values from -5 to 5
- key_heads: bfloat16 [4096, 4, 128], P('ctx', 'kv'), may hold values from -5 to 5
- value_head_rows: bfloat16 [4096, 4, 128], P('ctx', 'kv'), may hold values from -6 to 6
- out_grad: bfloat16 [4096, 32, 128], P('ctx', 'kv'), may hold values from -96 to 96
- doc_start: int32 [4096], P(('ctx', 'kv')), may hold values from 0 to 4095, as said below
Outputs:
- query_grad: bfloat16 [4096, 32, 128], P('ctx', 'kv')
- key_grad: bfloat16 [4096, 4, 128], P('ctx', 'kv')
- value_grad: bfloat16 [4096, 4, 128], P('ctx', 'kv')
Inputs may be any that keep to these rules, and one draw needn't show every extreme that they name: doc_start[p] is the first position of the document holding p: doc_start[p] <= p, and doc_start[p] equals p or doc_start[p - 1]; the last position starts a document of its own.
All inputs are finite; a program needn't handle non-finite values.
Results may differ from a plain program's by a relative error of at most 0.04.
Values may be sent and summed in bfloat16 or wider, within the bound.
A program may use at most 192 MiB of HBM per device.

v0:
```python
import functools
import math

import jax
import jax.numpy as jnp
from jax import lax
from jax.experimental import pallas as pl
from jax.experimental.pallas import tpu as pltpu
from jax.sharding import PartitionSpec as P

SPAN = 4
FILL = -1e30
TILE = 512
MESH = pl.DeviceIdType.MESH
F32 = jnp.float32
BF16 = jnp.bfloat16


def dot(a, b, dims):
    return lax.dot_general(a, b, (dims, ((), ())), preferred_element_type=F32)


def kernel(
    ctx_size, kv_size, block, per_group, scale,
    q_ref, k_ref, v_ref, do_ref, doc_ref,
    dq_ref, dk_ref, dv_ref,
    kbuf, vbuf, docbuf, lower, probs, dprobs, top, total, rowdot, weight, shift,
    ktrans, dq_acc, dk_acc, dv_acc, dk_out, dv_out, dk_in, dv_in,
    send_k, recv_k, send_v, recv_v, send_d, recv_d, send_gk, recv_gk, send_gv, recv_gv,
):
    tiles = q_ref.shape[0] // TILE
    toks = TILE // per_group
    ctx = lax.axis_index("ctx")
    kv = lax.axis_index("kv")

    def ahead(steps):
        return {"ctx": lax.rem(ctx + steps + ctx_size, ctx_size)}

    def beside(steps):
        return {"kv": lax.rem(kv + steps, kv_size)}

    barrier = pltpu.get_barrier_semaphore()
    for steps in range(1, SPAN):
        for sign in (1, -1):
            pl.semaphore_signal(barrier, inc=1, device_id=ahead(sign * steps), device_id_type=MESH)
    for steps in range(1, kv_size):
        pl.semaphore_signal(barrier, inc=1, device_id=beside(steps), device_id_type=MESH)
    docbuf[kv] = doc_ref[...]
    pl.semaphore_wait(barrier, 2 * (SPAN - 1) + kv_size - 1)

    doc_copies = []
    for steps in range(1, kv_size):
        doc_copies.append(
            pltpu.make_async_remote_copy(
                src_ref=doc_ref, dst_ref=docbuf.at[kv],
                send_sem=send_d.at[steps - 1], recv_sem=recv_d.at[steps - 1],
                device_id=beside(steps), device_id_type=MESH,
            )
        )
        doc_copies[-1].start()
    kv_copies = []
    for steps in range(1, SPAN):
        pair = []
        for src, dst, send, recv in ((k_ref, kbuf, send_k, recv_k), (v_ref, vbuf, send_v, recv_v)):
            pair.append(
                pltpu.make_async_remote_copy(
                    src_ref=src, dst_ref=dst.at[steps - 1],
                    send_sem=send.at[steps - 1], recv_sem=recv.at[steps - 1],
                    device_id=ahead(steps), device_id_type=MESH,
                )
            )
            pair[-1].start()
        kv_copies.append(pair)

    ktrans[0] = k_ref[...].T
    for copy in doc_copies:
        copy.wait()
    per_dev = docbuf.shape[1]
    for tile in range(tiles):
        parts = []
        for piece in range(TILE // 128):
            row = tile * (TILE // 128) + piece
            parts.append(docbuf[row // per_dev, pl.ds(row % per_dev, 1), :])
        lower[tile] = jnp.concatenate(parts, axis=1) - ctx * block

    def rows_of(tile):
        return pl.ds(pl.multiple_of(tile * TILE, TILE), TILE)

    def forward(offset, keys, values, key_count, tile):
        rows = rows_of(tile)
        position = lax.broadcasted_iota(jnp.int32, (key_count, TILE), 0)
        allowed = position >= lower[tile] + offset * block
        if offset == 0:
            token = tile * toks + lax.broadcasted_iota(jnp.int32, (1, TILE), 1) // per_group
            allowed = allowed & (position <= token)
        raw = dot(keys[pl.ds(0, key_count), :], q_ref[rows, :], ((1,), (1,)))
        scores = jnp.where(allowed, raw, FILL)
        highest = jnp.max(scores, axis=0, keepdims=True)
        unscaled = jnp.exp((scores - highest) * scale)
        gradient = dot(values[pl.ds(0, key_count), :], do_ref[rows, :], ((1,), (1,)))
        top[offset, tile] = highest
        total[offset, tile] = jnp.sum(unscaled, axis=0, keepdims=True)
        rowdot[offset, tile] = jnp.sum(unscaled * gradient, axis=0, keepdims=True)
        probs[offset, tile, pl.ds(0, key_count), :] = unscaled.astype(BF16)
        dprobs[offset, tile, pl.ds(0, key_count), :] = gradient.astype(BF16)

    def backward(offset, keys, key_count, tile):
        rows = rows_of(tile)
        w = weight[offset, tile].astype(BF16)
        r = shift[tile].astype(BF16)
        prob = probs[offset, tile, pl.ds(0, key_count), :] * w
        score = prob * (dprobs[offset, tile, pl.ds(0, key_count), :] - r)
        dv_acc[pl.ds(0, key_count), :] += dot(prob, do_ref[rows, :], ((1,), (0,)))
        dk_acc[pl.ds(0, key_count), :] += dot(score, q_ref[rows, :], ((1,), (0,)))
        part = dot(ktrans[offset, :, pl.ds(0, key_count)], score, ((1,), (0,)))
        if offset == SPAN - 1:
            dq_acc[tile] = part
        elif offset > 0:
            dq_acc[tile] += part
        else:
            dq_ref[rows, :] = ((dq_acc[tile] + part) * scale).T.astype(BF16)

    def over(first, last, body):
        def step(tile, carry):
            body(tile)
            return carry

        lax.fori_loop(first, last, step, 0)

    def over_own(body):
        half = tiles // 2
        over(0, half, functools.partial(body, block // 2))
        over(half, tiles, functools.partial(body, block))

    over_own(functools.partial(forward, 0, k_ref, v_ref))
    for offset in range(1, SPAN):
        for copy in kv_copies[offset - 1]:
            copy.wait()
        ktrans[offset] = kbuf[offset - 1].T
        over(0, tiles, functools.partial(forward, offset, kbuf.at[offset - 1], vbuf.at[offset - 1], block))

    def combine(tile):
        highest = top[0, tile]
        for offset in range(1, SPAN):
            highest = jnp.maximum(highest, top[offset, tile])
        factors = [jnp.exp((top[offset, tile] - highest) * scale) for offset in range(SPAN)]
        summed = factors[0] * total[0, tile]
        dotted = factors[0] * rowdot[0, tile]
        for offset in range(1, SPAN):
            summed += factors[offset] * total[offset, tile]
            dotted += factors[offset] * rowdot[offset, tile]
        inverse = 1.0 / summed
        shift[tile] = dotted * inverse
        for offset in range(SPAN):
            weight[offset, tile] = factors[offset] * inverse

    over(0, tiles, combine)

    grad_copies = []
    for offset in range(SPAN - 1, 0, -1):
        dk_acc[...] = jnp.zeros_like(dk_acc)
        dv_acc[...] = jnp.zeros_like(dv_acc)
        over(0, tiles, functools.partial(backward, offset, kbuf.at[offset - 1], block))
        slot = offset - 1
        dv_out[slot] = dv_acc[...].astype(BF16)
        dk_out[slot] = (dk_acc[...] * scale).astype(BF16)
        for src, dst, send, recv in (
            (dv_out, dv_in, send_gv, recv_gv),
            (dk_out, dk_in, send_gk, recv_gk),
        ):
            copy = pltpu.make_async_remote_copy(
                src_ref=src.at[slot], dst_ref=dst.at[slot],
                send_sem=send.at[slot], recv_sem=recv.at[slot],
                device_id=ahead(-offset), device_id_type=MESH,
            )
            copy.start()
            grad_copies.append(copy)
    dk_acc[...] = jnp.zeros_like(dk_acc)
    dv_acc[...] = jnp.zeros_like(dv_acc)
    over_own(functools.partial(backward, 0, k_ref))
    for copy in grad_copies:
        copy.wait()
    value = dv_acc[...]
    key = dk_acc[...] * scale
    for slot in range(SPAN - 1):
        value += dv_in[slot].astype(F32)
        key += dk_in[slot].astype(F32)
    dv_ref[...] = value.astype(BF16)
    dk_ref[...] = key.astype(BF16)


def local(ctx_size, kv_size, queries, key_heads, value_head_rows, out_grad, doc_start):
    block, heads, width = queries.shape
    rows = block * heads
    tiles = rows // TILE
    scale = 1.0 / math.sqrt(width)
    doc = jnp.repeat(doc_start, heads).reshape(-1, 128)
    vmem = pl.BlockSpec(memory_space=pltpu.VMEM)
    stat = (SPAN, tiles, 1, TILE)
    query_grad, key_grad, value_grad = pl.pallas_call(
        functools.partial(kernel, ctx_size, kv_size, block, heads, scale),
        out_shape=[
            jax.ShapeDtypeStruct((rows, width), BF16),
            jax.ShapeDtypeStruct((block, width), BF16),
            jax.ShapeDtypeStruct((block, width), BF16),
        ],
        in_specs=[vmem] * 5,
        out_specs=[vmem] * 3,
        scratch_shapes=[
            pltpu.VMEM((SPAN - 1, block, width), BF16),
            pltpu.VMEM((SPAN - 1, block, width), BF16),
            pltpu.VMEM((kv_size,) + doc.shape, jnp.int32),
            pltpu.VMEM((tiles, 1, TILE), jnp.int32),
            pltpu.VMEM((SPAN, tiles, block, TILE), BF16),
            pltpu.VMEM((SPAN, tiles, block, TILE), BF16),
            pltpu.VMEM(stat, F32),
            pltpu.VMEM(stat, F32),
            pltpu.VMEM(stat, F32),
            pltpu.VMEM(stat, F32),
            pltpu.VMEM(stat[1:], F32),
            pltpu.VMEM((SPAN, width, block), BF16),
            pltpu.VMEM((tiles, width, TILE), F32),
            pltpu.VMEM((block, width), F32),
            pltpu.VMEM((block, width), F32),
            pltpu.VMEM((SPAN - 1, block, width), BF16),
            pltpu.VMEM((SPAN - 1, block, width), BF16),
            pltpu.VMEM((SPAN - 1, block, width), BF16),
            pltpu.VMEM((SPAN - 1, block, width), BF16),
        ]
        + [pltpu.SemaphoreType.DMA((SPAN - 1,))] * 4
        + [pltpu.SemaphoreType.DMA((kv_size - 1,))] * 2
        + [pltpu.SemaphoreType.DMA((SPAN - 1,))] * 4,
        compiler_params=pltpu.CompilerParams(
            collective_id=0, has_side_effects=True, vmem_limit_bytes=56 * 1024 * 1024
        ),
        cost_estimate=pl.CostEstimate(
            flops=10 * rows * SPAN * block * width,
            bytes_accessed=8 * rows * width,
            transcendentals=rows * SPAN * block,
        ),
        name="attention_backward",
    )(
        queries.reshape(rows, width),
        key_heads.reshape(block, width),
        value_head_rows.reshape(block, width),
        out_grad.reshape(rows, width),
        doc,
    )
    return (
        query_grad.reshape(queries.shape),
        key_grad.reshape(key_heads.shape),
        value_grad.reshape(value_head_rows.shape),
    )


def solution(mesh):
    return jax.shard_map(
        functools.partial(local, mesh.shape["ctx"], mesh.shape["kv"]),
        mesh=mesh,
        in_specs=(
            P("ctx", "kv", None),
            P("ctx", "kv", None),
            P("ctx", "kv", None),
            P("ctx", "kv", None),
            P(("ctx", "kv")),
        ),
        out_specs=(P("ctx", "kv", None), P("ctx", "kv", None), P("ctx", "kv", None)),
        check_vma=False,
    )
```

profile of v0, /device:TPU:3, one launch (start us, length us, event | category | flops | bytes accessed | tf_op | source)
XLA Modules:
  0.0 56.0 jit_solution(15002108081063542813)
XLA Ops:
  0.6 0.0 copy-start.2
  0.6 0.6 %copy-done.2 = s32[128]{0:T(128)S(1)} copy-done((s32[128]{0:T(128)S(1)}, s32[128]{0:T(128)}, u32[]{:S(2)}) %copy-start.2) | copy-done | bytes 536
  1.3 0.1 broadcast_in_dim.7
  1.4 0.1 broadcast_in_dim.8
  1.4 0.7 %broadcast_in_dim.9.doc_ref = s32[8,128]{1,0:T(8,128)} reshape(s32[8,16,8]{2,1,0:T(8,128)S(1)} %broadcast_in_dim.8) | data formatting | bytes 8192 | tf_op jit(solution)/shard_map/broadcast_in_dim | solution.py:197
  2.1 49.9 %attention_backward.1 = (bf16[4096,128]{1,0:T(8,128)(2,1)}, bf16[512,128]{1,0:T(8,128)(2,1)}, bf16[512,128]{1,0:T(8,128)(2,1)}) custom-call(bf16[4096,128]{1,0:T(8,128)(2,1)} %bitcast.10, bf16[512,128]{1,0:T(8,128)(2,1)} %bitcast.12, bf16[512,128]{1,0:T(8,128)(2,1)} %bitcast.13, bf16[4096,128]{1,0:T(8,128)(2,1)} %bitcast.11, s32[8,128]{1,0:T(8,128)} %broadcast_in_dim.9.doc_ref), custom_call_target="tpu_custom_call" | custom-call | flops 10737418240 | bytes 4194304 | tf_op jit(solution)/shard_map/attention_backward/pallas_call | solution.py:200
  52.1 0.0 copy-start.1
  52.1 2.3 %copy.11 = bf16[512,8,128]{2,1,0:T(8,128)(2,1)} copy(bf16[512,8,128]{2,1,0:T(8,128)(2,1)} %bitcast.7) | data formatting | bytes 2097152
  54.4 0.0 copy-done.1
  54.4 0.0 copy-start
  54.4 0.7 %copy.12 = bf16[512,1,128]{2,0,1:T(8,128)(2,1)} copy(bf16[512,1,128]{2,0,1:T(8,128)(2,1)S(1)} %bitcast.9) | data formatting | bytes 262144
  55.1 0.3 copy-done
  55.4 0.7 %copy.13 = bf16[512,1,128]{2,0,1:T(8,128)(2,1)} copy(bf16[512,1,128]{2,0,1:T(8,128)(2,1)S(1)} %bitcast.8) | data formatting | bytes 262144
Async XLA Ops:
  0.6 0.7 %copy-start.2 = (s32[128]{0:T(128)S(1)}, s32[128]{0:T(128)}, u32[]{:S(2)}) copy-start(s32[128]{0:T(128)} %param.9) | copy-start | bytes 1540
  52.1 2.3 %copy-start.1 = (bf16[512,128]{1,0:T(8,128)(2,1)S(1)}, bf16[512,128]{1,0:T(8,128)(2,1)}, u32[]{:S(2)}) copy-start(bf16[512,128]{1,0:T(8,128)(2,1)} %get-tuple-element.7) | copy-start | bytes 393220
  54.4 1.0 %copy-start = (bf16[512,128]{1,0:T(8,128)(2,1)S(1)}, bf16[512,128]{1,0:T(8,128)(2,1)}, u32[]{:S(2)}) copy-start(bf16[512,128]{1,0:T(8,128)(2,1)} %get-tuple-element.8) | copy-start | bytes 393220
where the time goes:
time: 56.2 us; the launch traced here: 56 us
  Pallas kernels  49.9 us (89%)
  local copies, waits for them, and re-layouts  5.41 us (10%)
  between operations  0.66 us (1%)
    pallas_call x1, Pallas kernels, local(): pl.pallas_call(functools.partial(kernel, ctx_size, kv_size, block, heads,...  49.9 us
    unnamed x9, local copies, waits for them, and re-layouts  4.56 us

commit v1 on v0

--- a/solution.py
+++ b/solution.py
@@ -30,6 +30,7 @@
 ):
     tiles = q_ref.shape[0] // TILE
     toks = TILE // per_group
+    base2 = scale * math.log2(math.e)
     ctx = lax.axis_index("ctx")
     kv = lax.axis_index("kv")
 
@@ -96,7 +97,7 @@
         raw = dot(keys[pl.ds(0, key_count), :], q_ref[rows, :], ((1,), (1,)))
         scores = jnp.where(allowed, raw, FILL)
         highest = jnp.max(scores, axis=0, keepdims=True)
-        unscaled = jnp.exp((scores - highest) * scale)
+        unscaled = jnp.exp2((scores - highest) * base2)
         gradient = dot(values[pl.ds(0, key_count), :], do_ref[rows, :], ((1,), (1,)))
         top[offset, tile] = highest
         total[offset, tile] = jnp.sum(unscaled, axis=0, keepdims=True)
@@ -121,11 +122,12 @@
             dq_ref[rows, :] = ((dq_acc[tile] + part) * scale).T.astype(BF16)
 
     def over(first, last, body):
-        def step(tile, carry):
-            body(tile)
+        def step(pair, carry):
+            body(first + 2 * pair)
+            body(first + 2 * pair + 1)
             return carry
 
-        lax.fori_loop(first, last, step, 0)
+        lax.fori_loop(0, (last - first) // 2, step, 0)
 
     def over_own(body):
         half = tiles // 2
@@ -143,7 +145,7 @@
         highest = top[0, tile]
         for offset in range(1, SPAN):
             highest = jnp.maximum(highest, top[offset, tile])
-        factors = [jnp.exp((top[offset, tile] - highest) * scale) for offset in range(SPAN)]
+        factors = [jnp.exp2((top[offset, tile] - highest) * base2) for offset in range(SPAN)]
         summed = factors[0] * total[0, tile]
         dotted = factors[0] * rowdot[0, tile]
         for offset in range(1, SPAN):
@@ -189,6 +191,17 @@
     dk_ref[...] = key.astype(BF16)
 
 
+def hand_over(dq_in, dk_in, dv_in, dq_out, dk_out, dv_out, sems):
+    rows = dq_in.shape[0] // 4
+    pairs = [(dq_in.at[pl.ds(i * rows, rows), :], dq_out.at[pl.ds(i * rows, rows), :]) for i in range(4)]
+    pairs += [(dk_in, dk_out), (dv_in, dv_out)]
+    copies = [pltpu.make_async_copy(src, dst, sems.at[i]) for i, (src, dst) in enumerate(pairs)]
+    for copy in copies:
+        copy.start()
+    for copy in copies:
+        copy.wait()
+
+
 def local(ctx_size, kv_size, queries, key_heads, value_head_rows, out_grad, doc_start):
     block, heads, width = queries.shape
     rows = block * heads
@@ -197,7 +210,7 @@
     doc = jnp.repeat(doc_start, heads).reshape(-1, 128)
     vmem = pl.BlockSpec(memory_space=pltpu.VMEM)
     stat = (SPAN, tiles, 1, TILE)
-    query_grad, key_grad, value_grad = pl.pallas_call(
+    results = pl.pallas_call(
         functools.partial(kernel, ctx_size, kv_size, block, heads, scale),
         out_shape=[
             jax.ShapeDtypeStruct((rows, width), BF16),
@@ -246,6 +259,14 @@
         out_grad.reshape(rows, width),
         doc,
     )
+    query_grad, key_grad, value_grad = pl.pallas_call(
+        hand_over,
+        out_shape=[jax.ShapeDtypeStruct(x.shape, x.dtype) for x in results],
+        in_specs=[pl.BlockSpec(memory_space=pl.ANY)] * 3,
+        out_specs=[pl.BlockSpec(memory_space=pl.ANY)] * 3,
+        scratch_shapes=[pltpu.SemaphoreType.DMA((6,))],
+        name="hand_over",
+    )(*results)
     return (
         query_grad.reshape(queries.shape),
         key_grad.reshape(key_heads.shape),

time: 56.2 us -> 90.2 us (1.60)
  Pallas kernels: 49.9 us -> 87.8 us
  local copies, waits for them, and re-layouts: 5.41 us -> 1.5 us
    pallas_call x0 -> x1, Pallas kernels: none -> 40.9 us  [local(): pl.pallas_call(hand_over, out_shape=[jax.ShapeDtypeStruct(x.shape, x.dtyp...]
    unnamed x9 -> x2, local copies, waits for them, and re-layouts: 4.56 us -> 0.65 us
    pallas_call x1, Pallas kernels: 49.9 us -> 47 us  [local(): pl.pallas_call(functools.partial(kernel, ctx_size, kv_size, block, heads,...]
where the time goes in v1:
time: 90.2 us; the launch traced here: 90 us
  Pallas kernels  87.8 us (97%)
  local copies, waits for them, and re-layouts  1.5 us (2%)
    pallas_call x1, Pallas kernels, local(): pl.pallas_call(functools.partial(kernel, ctx_size, kv_size, block, heads,...  47 us
    pallas_call x1, Pallas kernels, local(): pl.pallas_call(hand_over, out_shape=[jax.ShapeDtypeStruct(x.shape, x.dtyp...  40.9 us

profile of v1, /device:TPU:3, one launch (start us, length us, event | category | flops | bytes accessed | tf_op | source)
XLA Modules:
  0.0 90.0 jit_solution(3847620813662483311)
XLA Ops:
  0.6 0.0 copy-start
  0.6 0.6 copy-done
  1.3 0.1 broadcast_in_dim.7
  1.4 0.1 broadcast_in_dim.8
  1.4 0.7 broadcast_in_dim.9.doc_ref
  2.1 47.0 %attention_backward.1 = (bf16[4096,128]{1,0:T(8,128)(2,1)}, bf16[512,128]{1,0:T(8,128)(2,1)}, bf16[512,128]{1,0:T(8,128)(2,1)}) custom-call(bf16[4096,128]{1,0:T(8,128)(2,1)} %bitcast.7, bf16[512,128]{1,0:T(8,128)(2,1)} %bitcast.10, bf16[512,128]{1,0:T(8,128)(2,1)} %bitcast.11, bf16[4096,128]{1,0:T(8,128)(2,1)} %bitcast.8, s32[8,128]{1,0:T(8,128)} %broadcast_in_dim.9.doc_ref), custom_call_target="tpu_custom_call" | custom-call | flops 10737418240 | bytes 4194304 | tf_op jit(solution)/shard_map/attention_backward/pallas_call | solution.py:213
  49.1 40.9 %hand_over.1 = (bf16[4096,128]{1,0:T(8,128)(2,1)}, bf16[512,128]{1,0:T(8,128)(2,1)}, bf16[512,128]{1,0:T(8,128)(2,1)}) custom-call(bf16[4096,128]{1,0:T(8,128)(2,1)} %get-tuple-element.9.dq_in, bf16[512,128]{1,0:T(8,128)(2,1)} %get-tuple-element.10.dk_in, bf16[512,128]{1,0:T(8,128)(2,1)} %get-tuple-element.11.dv_in), custom_call_target="tpu_custom_call" | custom-call | tf_op jit(solution)/shard_map/hand_over/pallas_call | solution.py:262
Async XLA Ops:
  0.6 0.7 copy-start

commit v2 on v0

v2 whole, which is shorter than its diff:
```python
import functools
import math

import jax
import jax.numpy as jnp
from jax import lax
from jax.experimental import pallas as pl
from jax.experimental.pallas import tpu as pltpu
from jax.sharding import PartitionSpec as P

SPAN = 4
FILL = -1e30
TILE = 512
SUB = 128
LANES = 128
STEPS = 4
MESH = pl.DeviceIdType.MESH
F32 = jnp.float32
BF16 = jnp.bfloat16


def dot(a, b, dims):
    return lax.dot_general(a, b, (dims, ((), ())), preferred_element_type=F32)


def kernel(
    ctx_size, kv_size, block, per_group, scale,
    q_ref, k_ref, v_ref, do_ref, doc_ref,
    dq_ref, dk_ref, dv_ref,
    kbuf, vbuf, docbuf, lower, probs, dprobs, top, total, rowdot, weight, shift,
    ktrans, dq_acc, dk_acc, dv_acc, dk_out, dv_out, dk_in, dv_in,
    send_k, recv_k, send_v, recv_v, send_d, recv_d, send_gk, recv_gk, send_gv, recv_gv,
):
    tiles = q_ref.shape[0] // TILE
    toks = TILE // per_group
    subs = block // SUB
    base2 = scale * math.log2(math.e)
    ctx = lax.axis_index("ctx")
    kv = lax.axis_index("kv")
    odd = lax.rem(ctx, 2)

    def ahead(steps):
        return {"ctx": lax.rem(ctx + steps + ctx_size, ctx_size)}

    def beside(steps):
        return {"kv": lax.rem(kv + steps, kv_size)}

    partner = {"ctx": ctx + 1 - 2 * odd}

    barrier = pltpu.get_barrier_semaphore()
    for steps in (1, -1, 3, -3):
        pl.semaphore_signal(barrier, inc=1, device_id=ahead(steps), device_id_type=MESH)
    for steps in range(1, kv_size):
        pl.semaphore_signal(barrier, inc=1, device_id=beside(steps), device_id_type=MESH)
    docbuf[kv] = doc_ref[...]
    pl.semaphore_wait(barrier, 4 + kv_size - 1)

    doc_copies = []
    for steps in range(1, kv_size):
        doc_copies.append(
            pltpu.make_async_remote_copy(
                src_ref=doc_ref, dst_ref=docbuf.at[kv],
                send_sem=send_d.at[steps - 1], recv_sem=recv_d.at[steps - 1],
                device_id=beside(steps), device_id_type=MESH,
            )
        )
        doc_copies[-1].start()

    def both(sources, targets, slot, sends, recvs, device):
        return [
            pltpu.make_async_remote_copy(
                src_ref=src, dst_ref=dst.at[slot],
                send_sem=send.at[slot], recv_sem=recv.at[slot],
                device_id=device, device_id_type=MESH,
            )
            for src, dst, send, recv in zip(sources, targets, sends, recvs)
        ]

    def start(copies):
        for copy in copies:
            copy.start()

    def received(copies):
        for copy in copies:
            copy.wait_recv()

    kv_buffers = ((kbuf, vbuf), (send_k, send_v), (recv_k, recv_v))
    one, three = [
        both((k_ref, v_ref), kv_buffers[0], steps - 1, kv_buffers[1], kv_buffers[2], ahead(steps))
        for steps in (1, 3)
    ]
    start(one)
    start(three)
    passed_on = both(
        (kbuf.at[2 * odd], vbuf.at[2 * odd]), kv_buffers[0], 1, kv_buffers[1], kv_buffers[2], partner
    )

    ktrans[0] = k_ref[...].T
    top[...] = jnp.full_like(top, FILL)
    total[...] = jnp.zeros_like(total)
    rowdot[...] = jnp.zeros_like(rowdot)
    for copy in doc_copies:
        copy.wait()
    per_dev = docbuf.shape[1]
    for tile in range(tiles):
        parts = []
        for piece in range(TILE // 128):
            row = tile * (TILE // 128) + piece
            parts.append(docbuf[row // per_dev, pl.ds(row % per_dev, 1), :])
        lower[tile] = jnp.concatenate(parts, axis=1) - ctx * block

    def rows_of(tile):
        return pl.ds(pl.multiple_of(tile * TILE, TILE), TILE)

    def forward(offset, keys, values, key_count, tile):
        rows = rows_of(tile)
        raw = dot(keys[pl.ds(0, key_count), :], q_ref[rows, :], ((1,), (1,)))
        gradient = dot(values[pl.ds(0, key_count), :], do_ref[rows, :], ((1,), (1,)))
        first = lower[tile] + offset * block
        position = lax.broadcasted_iota(jnp.int32, (SUB, LANES), 0)
        lane_token = lax.broadcasted_iota(jnp.int32, (1, LANES), 1) // per_group
        for lane in range(0, TILE, LANES):
            lanes = slice(lane, lane + LANES)
            for sub in range(key_count // SUB):
                part = slice(sub * SUB, (sub + 1) * SUB)
                allowed = position >= first[:, lanes] - sub * SUB
                if offset == 0:
                    token = lane_token + (tile * toks + lane // per_group - sub * SUB)
                    allowed = allowed & (position <= token)
                scores = jnp.where(allowed, raw[part, lanes], FILL)
                highest = jnp.max(scores, axis=0, keepdims=True)
                unscaled = jnp.exp2((scores - highest) * base2)
                line = pl.ds(offset * subs + sub, 1)
                chunk = gradient[part, lanes]
                top[tile, line, lanes] = highest
                total[tile, line, lanes] = jnp.sum(unscaled, axis=0, keepdims=True)
                rowdot[tile, line, lanes] = jnp.sum(unscaled * chunk, axis=0, keepdims=True)
                probs[offset, tile, pl.ds(sub * SUB, SUB), lanes] = unscaled.astype(BF16)
                dprobs[offset, tile, pl.ds(sub * SUB, SUB), lanes] = chunk.astype(BF16)

    def backward(offset, first, keys, key_count, tile):
        rows = rows_of(tile)
        r = shift[tile].astype(BF16)
        prob_parts = []
        score_parts = []
        for sub in range(key_count // SUB):
            part = pl.ds(sub * SUB, SUB)
            w = weight[tile, pl.ds(offset * subs + sub, 1), :].astype(BF16)
            prob_parts.append(probs[offset, tile, part, :] * w)
            score_parts.append(prob_parts[-1] * (dprobs[offset, tile, part, :] - r))
        prob = jnp.concatenate(prob_parts, axis=0)
        score = jnp.concatenate(score_parts, axis=0)
        dv_acc[pl.ds(0, key_count), :] += dot(prob, do_ref[rows, :], ((1,), (0,)))
        dk_acc[pl.ds(0, key_count), :] += dot(score, q_ref[rows, :], ((1,), (0,)))
        part = dot(ktrans[offset, :, pl.ds(0, key_count)], score, ((1,), (0,)))
        if first:
            dq_acc[tile] = part
        elif offset > 0:
            dq_acc[tile] += part
        else:
            dq_ref[rows, :] = ((dq_acc[tile] + part) * scale).T.astype(BF16)

    def over(body):
        def step(pair, carry):
            body(2 * pair)
            body(2 * pair + 1)
            return carry

        lax.fori_loop(0, tiles // 2, step, 0)

    def over_own(body):
        for tile in range(tiles):
            body(SUB * (((tile + 1) * toks + SUB - 1) // SUB), tile)

    def visit(offset):
        ktrans[offset] = kbuf[offset - 1].T
        over(functools.partial(forward, offset, kbuf.at[offset - 1], vbuf.at[offset - 1], block))

    over_own(functools.partial(forward, 0, k_ref, v_ref))
    received(one)

    @pl.when(odd == 0)
    def _():
        start(passed_on)

    visit(1)
    received(three)

    @pl.when(odd == 1)
    def _():
        start(passed_on)

    visit(3)
    received(passed_on)
    visit(2)

    def combine(tile):
        tops = top[tile]
        factors = jnp.exp2((tops - jnp.max(tops, axis=0, keepdims=True)) * base2)
        inverse = 1.0 / jnp.sum(factors * total[tile], axis=0, keepdims=True)
        shift[tile] = jnp.sum(factors * rowdot[tile], axis=0, keepdims=True) * inverse
        weight[tile] = factors * inverse

    over(combine)

    def accumulate(offset, first):
        dk_acc[...] = jnp.zeros_like(dk_acc)
        dv_acc[...] = jnp.zeros_like(dv_acc)
        over(functools.partial(backward, offset, first, kbuf.at[offset - 1], block))
        dk_acc[...] = dk_acc[...] * scale

    grad_sends, grad_recvs = (send_gk, send_gv), (recv_gk, recv_gv)

    def give(offset, device):
        slot = offset - 1
        dk_out[slot] = dk_acc[...].astype(BF16)
        dv_out[slot] = dv_acc[...].astype(BF16)
        copies = both(
            (dk_out.at[slot], dv_out.at[slot]), (dk_in, dv_in), slot, grad_sends, grad_recvs, device
        )
        start(copies)
        return copies

    def take(slot):
        dk_acc[...] += dk_in[slot].astype(F32)
        dv_acc[...] += dv_in[slot].astype(F32)

    accumulate(2, True)
    given_two = give(2, partner)
    accumulate(3, False)

    @pl.when(odd == 1)
    def _():
        received(given_two)
        take(1)

    given_three = give(3, ahead(-3))
    accumulate(1, False)

    @pl.when(odd == 0)
    def _():
        received(given_two)
        take(1)

    given_one = give(1, ahead(-1))
    dk_acc[...] = jnp.zeros_like(dk_acc)
    dv_acc[...] = jnp.zeros_like(dv_acc)
    over_own(functools.partial(backward, 0, False, k_ref))
    dk_acc[...] = dk_acc[...] * scale
    received(given_three)
    take(2)
    received(given_one)
    take(0)
    dv_ref[...] = dv_acc[...].astype(BF16)
    dk_ref[...] = dk_acc[...].astype(BF16)
    for copies in (one, three, passed_on, given_two, given_three, given_one):
        for copy in copies:
            copy.wait_send()


def hand_over(dq_in, dk_in, dv_in, dq_out, dk_out, dv_out):
    dq_out[...] = dq_in[...]
    dk_out[...] = dk_in[...]
    dv_out[...] = dv_in[...]


def local(ctx_size, kv_size, queries, key_heads, value_head_rows, out_grad, doc_start):
    block, heads, width = queries.shape
    rows = block * heads
    tiles = rows // TILE
    scale = 1.0 / math.sqrt(width)
    doc = jnp.repeat(doc_start, heads).reshape(-1, 128)
    vmem = pl.BlockSpec(memory_space=pltpu.VMEM)
    stat = (tiles, SPAN * (block // SUB), TILE)
    results = pl.pallas_call(
        functools.partial(kernel, ctx_size, kv_size, block, heads, scale),
        out_shape=[
            jax.ShapeDtypeStruct((rows, width), BF16),
            jax.ShapeDtypeStruct((block, width), BF16),
            jax.ShapeDtypeStruct((block, width), BF16),
        ],
        in_specs=[vmem] * 5,
        out_specs=[vmem] * 3,
        scratch_shapes=[
            pltpu.VMEM((SPAN - 1, block, width), BF16),
            pltpu.VMEM((SPAN - 1, block, width), BF16),
            pltpu.VMEM((kv_size,) + doc.shape, jnp.int32),
            pltpu.VMEM((tiles, 1, TILE), jnp.int32),
            pltpu.VMEM((SPAN, tiles, block, TILE), BF16),
            pltpu.VMEM((SPAN, tiles, block, TILE), BF16),
            pltpu.VMEM(stat, F32),
            pltpu.VMEM(stat, F32),
            pltpu.VMEM(stat, F32),
            pltpu.VMEM(stat, F32),
            pltpu.VMEM((tiles, 1, TILE), F32),
            pltpu.VMEM((SPAN, width, block), BF16),
            pltpu.VMEM((tiles, width, TILE), F32),
            pltpu.VMEM((block, width), F32),
            pltpu.VMEM((block, width), F32),
            pltpu.VMEM((SPAN - 1, block, width), BF16),
            pltpu.VMEM((SPAN - 1, block, width), BF16),
            pltpu.VMEM((SPAN - 1, block, width), BF16),
            pltpu.VMEM((SPAN - 1, block, width), BF16),
        ]
        + [pltpu.SemaphoreType.DMA((SPAN - 1,))] * 4
        + [pltpu.SemaphoreType.DMA((kv_size - 1,))] * 2
        + [pltpu.SemaphoreType.DMA((SPAN - 1,))] * 4,
        compiler_params=pltpu.CompilerParams(
            collective_id=0, has_side_effects=True, vmem_limit_bytes=56 * 1024 * 1024
        ),
        cost_estimate=pl.CostEstimate(
            flops=10 * rows * SPAN * block * width,
            bytes_accessed=8 * rows * width,
            transcendentals=rows * SPAN * block,
        ),
        name="attention_backward",
    )(
        queries.reshape(rows, width),
        key_heads.reshape(block, width),
        value_head_rows.reshape(block, width),
        out_grad.reshape(rows, width),
        doc,
    )
    specs = [pl.BlockSpec((x.shape[0] // STEPS, width), lambda i: (i, 0)) for x in results]
    query_grad, key_grad, value_grad = pl.pallas_call(
        hand_over,
        out_shape=[jax.ShapeDtypeStruct(x.shape, x.dtype) for x in results],
        grid=(STEPS,),
        in_specs=specs,
        out_specs=specs,
        name="hand_over",
    )(*results)
    return (
        query_grad.reshape(queries.shape),
        key_grad.reshape(key_heads.shape),
        value_grad.reshape(value_head_rows.shape),
    )


def solution(mesh):
    return jax.shard_map(
        functools.partial(local, mesh.shape["ctx"], mesh.shape["kv"]),
        mesh=mesh,
        in_specs=(
            P("ctx", "kv", None),
            P("ctx", "kv", None),
            P("ctx", "kv", None),
            P("ctx", "kv", None),
            P(("ctx", "kv")),
        ),
        out_specs=(P("ctx", "kv", None), P("ctx", "kv", None), P("ctx", "kv", None)),
        check_vma=False,
    )
```

time: 56.2 us -> 51 us (0.907)
  local copies, waits for them, and re-layouts: 5.41 us -> 1.5 us
  Pallas kernels: 49.9 us -> 48.6 us
    pallas_call x1, Pallas kernels: 49.9 us -> 45.2 us  [local(): pl.pallas_call(functools.partial(kernel, ctx_size, kv_size, block, heads,...]
    unnamed x9 -> x2, local copies, waits for them, and re-layouts: 4.56 us -> 0.65 us
    pallas_call x0 -> x1, Pallas kernels: none -> 3.46 us  [local(): pl.pallas_call(hand_over, out_shape=[jax.ShapeDtypeStruct(x.shape, x.dtyp...]
where the time goes in v2:
time: 51 us; the launch traced here: 50.8 us
  Pallas kernels  48.6 us (95%)
  local copies, waits for them, and re-layouts  1.5 us (3%)
  between operations  0.65 us (1%)
    pallas_call x1, Pallas kernels, local(): pl.pallas_call(functools.partial(kernel, ctx_size, kv_size, block, heads,...  45.2 us
    pallas_call x1, Pallas kernels, local(): pl.pallas_call(hand_over, out_shape=[jax.ShapeDtypeStruct(x.shape, x.dtyp...  3.46 us

profile of v2, /device:TPU:3, one launch (start us, length us, event | category | flops | bytes accessed | tf_op | source)
XLA Modules:
  0.0 50.8 jit_solution(10587354267257358685)
XLA Ops:
  0.6 0.0 copy-start
  0.6 0.6 %copy-done = s32[128]{0:T(128)S(1)} copy-done((s32[128]{0:T(128)S(1)}, s32[128]{0:T(128)}, u32[]{:S(2)}) %copy-start) | copy-done | bytes 536
  1.3 0.1 broadcast_in_dim.7
  1.4 0.1 broadcast_in_dim.8
  1.4 0.7 %broadcast_in_dim.9.doc_ref = s32[8,128]{1,0:T(8,128)} reshape(s32[8,16,8]{2,1,0:T(8,128)S(1)} %broadcast_in_dim.8) | data formatting | bytes 8192 | tf_op jit(solution)/shard_map/broadcast_in_dim | solution.py:272
  2.1 45.2 %attention_backward.1 = (bf16[4096,128]{1,0:T(8,128)(2,1)}, bf16[512,128]{1,0:T(8,128)(2,1)}, bf16[512,128]{1,0:T(8,128)(2,1)}) custom-call(bf16[4096,128]{1,0:T(8,128)(2,1)} %bitcast.7, bf16[512,128]{1,0:T(8,128)(2,1)} %bitcast.10, bf16[512,128]{1,0:T(8,128)(2,1)} %bitcast.11, bf16[4096,128]{1,0:T(8,128)(2,1)} %bitcast.8, s32[8,128]{1,0:T(8,128)} %broadcast_in_dim.9.doc_ref), custom_call_target="tpu_custom_call" | custom-call | flops 10737418240 | bytes 4194304 | tf_op jit(solution)/shard_map/attention_backward/pallas_call | solution.py:275
  47.3 3.5 %hand_over.1 = (bf16[4096,128]{1,0:T(8,128)(2,1)}, bf16[512,128]{1,0:T(8,128)(2,1)}, bf16[512,128]{1,0:T(8,128)(2,1)}) custom-call(bf16[4096,128]{1,0:T(8,128)(2,1)} %get-tuple-element.9.dq_in, bf16[512,128]{1,0:T(8,128)(2,1)} %get-tuple-element.10.dk_in, bf16[512,128]{1,0:T(8,128)(2,1)} %get-tuple-element.11.dv_in), custom_call_target="tpu_custom_call" | custom-call | tf_op jit(solution)/shard_map/hand_over/pallas_call | solution.py:325
Async XLA Ops:
  0.6 0.7 %copy-start = (s32[128]{0:T(128)S(1)}, s32[128]{0:T(128)}, u32[]{:S(2)}) copy-start(s32[128]{0:T(128)} %param.9) | copy-start | bytes 1540

commit v3 on v2

--- a/solution.py
+++ b/solution.py
@@ -13,6 +13,7 @@
 TILE = 512
 SUB = 128
 LANES = 128
+HALF = 256
 STEPS = 4
 MESH = pl.DeviceIdType.MESH
 F32 = jnp.float32
@@ -25,11 +26,13 @@
 
 def kernel(
     ctx_size, kv_size, block, per_group, scale,
-    q_ref, k_ref, v_ref, do_ref, doc_ref,
-    dq_ref, dk_ref, dv_ref,
+    q_any, k_any, v_any, do_any, doc_any,
+    dq_any, dk_ref, dv_ref,
+    q_ref, k_ref, v_ref, do_ref, dq_ref, s_even, s_odd, p_even, p_odd,
     kbuf, vbuf, docbuf, lower, probs, dprobs, top, total, rowdot, weight, shift,
     ktrans, dq_acc, dk_acc, dv_acc, dk_out, dv_out, dk_in, dv_in,
     send_k, recv_k, send_v, recv_v, send_d, recv_d, send_gk, recv_gk, send_gv, recv_gv,
+    load_sem, store_sem,
 ):
     tiles = q_ref.shape[0] // TILE
     toks = TILE // per_group
@@ -45,6 +48,18 @@
     def beside(steps):
         return {"kv": lax.rem(kv + steps, kv_size)}
 
+    loads = [
+        pltpu.make_async_copy(src, dst, load_sem.at[i])
+        for i, (src, dst) in enumerate(
+            (
+                (doc_any, docbuf.at[kv]), (k_any, k_ref), (q_any, q_ref),
+                (v_any, v_ref), (do_any, do_ref),
+            )
+        )
+    ]
+    for copy in loads:
+        copy.start()
+
     partner = {"ctx": ctx + 1 - 2 * odd}
 
     barrier = pltpu.get_barrier_semaphore()
@@ -52,14 +67,13 @@
         pl.semaphore_signal(barrier, inc=1, device_id=ahead(steps), device_id_type=MESH)
     for steps in range(1, kv_size):
         pl.semaphore_signal(barrier, inc=1, device_id=beside(steps), device_id_type=MESH)
-    docbuf[kv] = doc_ref[...]
     pl.semaphore_wait(barrier, 4 + kv_size - 1)
 
     doc_copies = []
     for steps in range(1, kv_size):
         doc_copies.append(
             pltpu.make_async_remote_copy(
-                src_ref=doc_ref, dst_ref=docbuf.at[kv],
+                src_ref=doc_any, dst_ref=docbuf.at[kv],
                 send_sem=send_d.at[steps - 1], recv_sem=recv_d.at[steps - 1],
                 device_id=beside(steps), device_id_type=MESH,
             )
@@ -86,7 +100,7 @@
 
     kv_buffers = ((kbuf, vbuf), (send_k, send_v), (recv_k, recv_v))
     one, three = [
-        both((k_ref, v_ref), kv_buffers[0], steps - 1, kv_buffers[1], kv_buffers[2], ahead(steps))
+        both((k_any, v_any), kv_buffers[0], steps - 1, kv_buffers[1], kv_buffers[2], ahead(steps))
         for steps in (1, 3)
     ]
     start(one)
@@ -95,6 +109,8 @@
         (kbuf.at[2 * odd], vbuf.at[2 * odd]), kv_buffers[0], 1, kv_buffers[1], kv_buffers[2], partner
     )
 
+    for copy in loads:
+        copy.wait()
     ktrans[0] = k_ref[...].T
     top[...] = jnp.full_like(top, FILL)
     total[...] = jnp.zeros_like(total)
@@ -112,31 +128,48 @@
     def rows_of(tile):
         return pl.ds(pl.multiple_of(tile * TILE, TILE), TILE)
 
-    def forward(offset, keys, values, key_count, tile):
-        rows = rows_of(tile)
-        raw = dot(keys[pl.ds(0, key_count), :], q_ref[rows, :], ((1,), (1,)))
-        gradient = dot(values[pl.ds(0, key_count), :], do_ref[rows, :], ((1,), (1,)))
+    def products(keys, values, key_count, tile, lane, held):
+        s_ref, p_ref = held
+        rows = pl.ds(pl.multiple_of(tile * TILE + lane, HALF), HALF)
+        lanes = slice(lane, lane + HALF)
+        count = pl.ds(0, key_count)
+        s_ref[count, lanes] = dot(keys[count, :], q_ref[rows, :], ((1,), (1,)))
+        p_ref[count, lanes] = dot(values[count, :], do_ref[rows, :], ((1,), (1,))).astype(BF16)
+
+    def softmax(offset, key_count, tile, start_lane, held):
+        s_ref, p_ref = held
         first = lower[tile] + offset * block
         position = lax.broadcasted_iota(jnp.int32, (SUB, LANES), 0)
         lane_token = lax.broadcasted_iota(jnp.int32, (1, LANES), 1) // per_group
-        for lane in range(0, TILE, LANES):
+        for lane in range(start_lane, start_lane + HALF, LANES):
             lanes = slice(lane, lane + LANES)
             for sub in range(key_count // SUB):
-                part = slice(sub * SUB, (sub + 1) * SUB)
+                part = pl.ds(sub * SUB, SUB)
                 allowed = position >= first[:, lanes] - sub * SUB
                 if offset == 0:
                     token = lane_token + (tile * toks + lane // per_group - sub * SUB)
                     allowed = allowed & (position <= token)
-                scores = jnp.where(allowed, raw[part, lanes], FILL)
+                scores = jnp.where(allowed, s_ref[part, lanes], FILL)
                 highest = jnp.max(scores, axis=0, keepdims=True)
                 unscaled = jnp.exp2((scores - highest) * base2)
                 line = pl.ds(offset * subs + sub, 1)
-                chunk = gradient[part, lanes]
+                chunk = p_ref[part, lanes]
                 top[tile, line, lanes] = highest
                 total[tile, line, lanes] = jnp.sum(unscaled, axis=0, keepdims=True)
-                rowdot[tile, line, lanes] = jnp.sum(unscaled * chunk, axis=0, keepdims=True)
-                probs[offset, tile, pl.ds(sub * SUB, SUB), lanes] = unscaled.astype(BF16)
-                dprobs[offset, tile, pl.ds(sub * SUB, SUB), lanes] = chunk.astype(BF16)
+                rowdot[tile, line, lanes] = jnp.sum(
+                    unscaled * chunk.astype(F32), axis=0, keepdims=True
+                )
+                probs[offset, tile, part, lanes] = unscaled.astype(BF16)
+                dprobs[offset, tile, part, lanes] = chunk
+
+    def forward(offset, keys, values, now, later):
+        tile, count, held = now
+        for lane in range(0, TILE, HALF):
+            if later is not None:
+                products(keys, values, later[1], later[0], lane, later[2])
+            softmax(offset, count, tile, lane, held)
+
+    even, unequal = (s_even, p_even), (s_odd, p_odd)
 
     def backward(offset, first, keys, key_count, tile):
         rows = rows_of(tile)
@@ -159,6 +192,14 @@
             dq_acc[tile] += part
         else:
             dq_ref[rows, :] = ((dq_acc[tile] + part) * scale).T.astype(BF16)
+            stores[tile].start()
+
+    stores = [
+        pltpu.make_async_copy(
+            dq_ref.at[pl.ds(tile * TILE, TILE), :], dq_any.at[pl.ds(tile * TILE, TILE), :], store_sem.at[tile]
+        )
+        for tile in range(tiles)
+    ]
 
     def over(body):
         def step(pair, carry):
@@ -173,10 +214,26 @@
             body(SUB * (((tile + 1) * toks + SUB - 1) // SUB), tile)
 
     def visit(offset):
-        ktrans[offset] = kbuf[offset - 1].T
-        over(functools.partial(forward, offset, kbuf.at[offset - 1], vbuf.at[offset - 1], block))
-
-    over_own(functools.partial(forward, 0, k_ref, v_ref))
+        keys, values = kbuf.at[offset - 1], vbuf.at[offset - 1]
+        ktrans[offset] = keys[...].T
+        for lane in range(0, TILE, HALF):
+            products(keys, values, block, 0, lane, even)
+
+        def step(pair, carry):
+            tile = 2 * pair
+            after = jnp.minimum(tile + 2, tiles - 1)
+            forward(offset, keys, values, (tile, block, even), (tile + 1, block, unequal))
+            forward(offset, keys, values, (tile + 1, block, unequal), (after, block, even))
+            return carry
+
+        lax.fori_loop(0, tiles // 2, step, 0)
+
+    own = []
+    over_own(lambda count, tile: own.append((tile, count, (even, unequal)[tile % 2])))
+    for lane in range(0, TILE, HALF):
+        products(k_ref, v_ref, own[0][1], 0, lane, even)
+    for now, later in zip(own, own[1:] + [None]):
+        forward(0, k_ref, v_ref, now, later)
     received(one)
 
     @pl.when(odd == 0)
@@ -256,12 +313,25 @@
     for copies in (one, three, passed_on, given_two, given_three, given_one):
         for copy in copies:
             copy.wait_send()
-
-
-def hand_over(dq_in, dk_in, dv_in, dq_out, dk_out, dv_out):
-    dq_out[...] = dq_in[...]
-    dk_out[...] = dk_in[...]
-    dv_out[...] = dv_in[...]
+    for copy in stores:
+        copy.wait()
+
+
+def hand_over(dq_in, dk_in, dv_in, dq_out, dk_out, dv_out, dq_mid, dk_mid, dv_mid, sems):
+    parts = [(dk_in, dk_mid, dk_out), (dv_in, dv_mid, dv_out)]
+    rows = dq_in.shape[0] // STEPS
+    for step in range(STEPS):
+        part = pl.ds(step * rows, rows)
+        parts.append((dq_in.at[part, :], dq_mid.at[part, :], dq_out.at[part, :]))
+    fetches = [pltpu.make_async_copy(a, b, sems.at[0, i]) for i, (a, b, _) in enumerate(parts)]
+    stores = [pltpu.make_async_copy(b, c, sems.at[1, i]) for i, (_, b, c) in enumerate(parts)]
+    for fetch in fetches:
+        fetch.start()
+    for fetch, store in zip(fetches, stores):
+        fetch.wait()
+        store.start()
+    for store in stores:
+        store.wait()
 
 
 def local(ctx_size, kv_size, queries, key_heads, value_head_rows, out_grad, doc_start):
@@ -279,9 +349,18 @@
             jax.ShapeDtypeStruct((block, width), BF16),
             jax.ShapeDtypeStruct((block, width), BF16),
         ],
-        in_specs=[vmem] * 5,
-        out_specs=[vmem] * 3,
+        in_specs=[pl.BlockSpec(memory_space=pl.ANY)] * 5,
+        out_specs=[pl.BlockSpec(memory_space=pl.ANY), vmem, vmem],
         scratch_shapes=[
+            pltpu.VMEM((rows, width), BF16),
+            pltpu.VMEM((block, width), BF16),
+            pltpu.VMEM((block, width), BF16),
+            pltpu.VMEM((rows, width), BF16),
+            pltpu.VMEM((rows, width), BF16),
+            pltpu.VMEM((block, TILE), F32),
+            pltpu.VMEM((block, TILE), F32),
+            pltpu.VMEM((block, TILE), BF16),
+            pltpu.VMEM((block, TILE), BF16),
             pltpu.VMEM((SPAN - 1, block, width), BF16),
             pltpu.VMEM((SPAN - 1, block, width), BF16),
             pltpu.VMEM((kv_size,) + doc.shape, jnp.int32),
@@ -304,7 +383,8 @@
         ]
         + [pltpu.SemaphoreType.DMA((SPAN - 1,))] * 4
         + [pltpu.SemaphoreType.DMA((kv_size - 1,))] * 2
-        + [pltpu.SemaphoreType.DMA((SPAN - 1,))] * 4,
+        + [pltpu.SemaphoreType.DMA((SPAN - 1,))] * 4
+        + [pltpu.SemaphoreType.DMA((5,)), pltpu.SemaphoreType.DMA((tiles,))],
         compiler_params=pltpu.CompilerParams(
             collective_id=0, has_side_effects=True, vmem_limit_bytes=56 * 1024 * 1024
         ),
@@ -321,13 +401,14 @@
         out_grad.reshape(rows, width),
         doc,
     )
-    specs = [pl.BlockSpec((x.shape[0] // STEPS, width), lambda i: (i, 0)) for x in results]
+    anywhere = pl.BlockSpec(memory_space=pl.ANY)
     query_grad, key_grad, value_grad = pl.pallas_call(
         hand_over,
         out_shape=[jax.ShapeDtypeStruct(x.shape, x.dtype) for x in results],
-        grid=(STEPS,),
-        in_specs=specs,
-        out_specs=specs,
+        in_specs=[anywhere] * 3,
+        out_specs=[anywhere] * 3,
+        scratch_shapes=[pltpu.VMEM(x.shape, x.dtype) for x in results]
+        + [pltpu.SemaphoreType.DMA((2, STEPS + 2))],
         name="hand_over",
     )(*results)
     return (

time: 51 us -> 52.5 us (1.029)
  Pallas kernels: 48.6 us -> 50.2 us
    pallas_call x1, Pallas kernels: 45.2 us -> 48 us  [local(): pl.pallas_call(functools.partial(kernel, ctx_size, kv_size, block, heads,...]
    pallas_call x1, Pallas kernels: 3.46 us -> 2.15 us  [local(): pl.pallas_call(hand_over, out_shape=[jax.ShapeDtypeStruct(x.shape, x.dtyp...]
where the time goes in v3:
time: 52.5 us; the launch traced here: 52.3 us
  Pallas kernels  50.2 us (96%)
  local copies, waits for them, and re-layouts  1.5 us (3%)
  between operations  0.65 us (1%)
    pallas_call x1, Pallas kernels, local(): pl.pallas_call(functools.partial(kernel, ctx_size, kv_size, block, heads,...  48 us
    pallas_call x1, Pallas kernels, local(): pl.pallas_call(hand_over, out_shape=[jax.ShapeDtypeStruct(x.shape, x.dtyp...  2.15 us

profile of v3, /device:TPU:3, one launch (start us, length us, event | category | flops | bytes accessed | tf_op | source)
XLA Modules:
  0.0 52.3 jit_solution(2080908789805871735)
XLA Ops:
  0.6 0.0 copy-start
  0.6 0.6 %copy-done = s32[128]{0:T(128)S(1)} copy-done((s32[128]{0:T(128)S(1)}, s32[128]{0:T(128)}, u32[]{:S(2)}) %copy-start) | copy-done | bytes 536
  1.3 0.1 broadcast_in_dim.7
  1.4 0.1 broadcast_in_dim.8
  1.4 0.7 %broadcast_in_dim.9.doc_any = s32[8,128]{1,0:T(8,128)} reshape(s32[8,16,8]{2,1,0:T(8,128)S(1)} %broadcast_in_dim.8) | data formatting | bytes 8192 | tf_op jit(solution)/shard_map/broadcast_in_dim | solution.py:342
  2.1 48.0 %attention_backward.1 = (bf16[4096,128]{1,0:T(8,128)(2,1)}, bf16[512,128]{1,0:T(8,128)(2,1)}, bf16[512,128]{1,0:T(8,128)(2,1)}) custom-call(bf16[4096,128]{1,0:T(8,128)(2,1)} %bitcast.7, bf16[512,128]{1,0:T(8,128)(2,1)} %bitcast.10, bf16[512,128]{1,0:T(8,128)(2,1)} %bitcast.11, bf16[4096,128]{1,0:T(8,128)(2,1)} %bitcast.8, s32[8,128]{1,0:T(8,128)} %broadcast_in_dim.9.doc_any), custom_call_target="tpu_custom_call" | custom-call | flops 10737418240 | bytes 4194304 | tf_op jit(solution)/shard_map/attention_backward/pallas_call | solution.py:345
  50.2 2.1 %hand_over.1 = (bf16[4096,128]{1,0:T(8,128)(2,1)}, bf16[512,128]{1,0:T(8,128)(2,1)}, bf16[512,128]{1,0:T(8,128)(2,1)}) custom-call(bf16[4096,128]{1,0:T(8,128)(2,1)} %get-tuple-element.9.dq_in, bf16[512,128]{1,0:T(8,128)(2,1)} %get-tuple-element.10.dk_in, bf16[512,128]{1,0:T(8,128)(2,1)} %get-tuple-element.11.dv_in), custom_call_target="tpu_custom_call" | custom-call | tf_op jit(solution)/shard_map/hand_over/pallas_call | solution.py:405
Async XLA Ops:
  0.6 0.7 %copy-start = (s32[128]{0:T(128)S(1)}, s32[128]{0:T(128)}, u32[]{:S(2)}) copy-start(s32[128]{0:T(128)} %param.9) | copy-start | bytes 1540

commit v4 on v3

--- a/solution.py
+++ b/solution.py
@@ -11,9 +11,9 @@
 SPAN = 4
 FILL = -1e30
 TILE = 512
-SUB = 128
+SUB = 256
+CUT = 128
 LANES = 128
-HALF = 256
 STEPS = 4
 MESH = pl.DeviceIdType.MESH
 F32 = jnp.float32
@@ -28,7 +28,7 @@
     ctx_size, kv_size, block, per_group, scale,
     q_any, k_any, v_any, do_any, doc_any,
     dq_any, dk_ref, dv_ref,
-    q_ref, k_ref, v_ref, do_ref, dq_ref, s_even, s_odd, p_even, p_odd,
+    q_ref, k_ref, v_ref, do_ref, dq_ref,
     kbuf, vbuf, docbuf, lower, probs, dprobs, top, total, rowdot, weight, shift,
     ktrans, dq_acc, dk_acc, dv_acc, dk_out, dv_out, dk_in, dv_in,
     send_k, recv_k, send_v, recv_v, send_d, recv_d, send_gk, recv_gk, send_gv, recv_gv,
@@ -128,59 +128,48 @@
     def rows_of(tile):
         return pl.ds(pl.multiple_of(tile * TILE, TILE), TILE)
 
-    def products(keys, values, key_count, tile, lane, held):
-        s_ref, p_ref = held
-        rows = pl.ds(pl.multiple_of(tile * TILE + lane, HALF), HALF)
-        lanes = slice(lane, lane + HALF)
-        count = pl.ds(0, key_count)
-        s_ref[count, lanes] = dot(keys[count, :], q_ref[rows, :], ((1,), (1,)))
-        p_ref[count, lanes] = dot(values[count, :], do_ref[rows, :], ((1,), (1,))).astype(BF16)
-
-    def softmax(offset, key_count, tile, start_lane, held):
-        s_ref, p_ref = held
+    def pieces(key_count):
+        return [(start, min(SUB, key_count - start)) for start in range(0, key_count, SUB)]
+
+    def forward(offset, keys, values, key_count, tile):
+        rows = rows_of(tile)
+        raw = dot(keys[pl.ds(0, key_count), :], q_ref[rows, :], ((1,), (1,)))
+        gradient = dot(values[pl.ds(0, key_count), :], do_ref[rows, :], ((1,), (1,)))
         first = lower[tile] + offset * block
-        position = lax.broadcasted_iota(jnp.int32, (SUB, LANES), 0)
         lane_token = lax.broadcasted_iota(jnp.int32, (1, LANES), 1) // per_group
-        for lane in range(start_lane, start_lane + HALF, LANES):
+        for lane in range(0, TILE, LANES):
             lanes = slice(lane, lane + LANES)
-            for sub in range(key_count // SUB):
-                part = pl.ds(sub * SUB, SUB)
-                allowed = position >= first[:, lanes] - sub * SUB
+            for start, size in pieces(key_count):
+                position = lax.broadcasted_iota(jnp.int32, (size, LANES), 0)
+                part = slice(start, start + size)
+                allowed = position >= first[:, lanes] - start
                 if offset == 0:
-                    token = lane_token + (tile * toks + lane // per_group - sub * SUB)
+                    token = lane_token + (tile * toks + lane // per_group - start)
                     allowed = allowed & (position <= token)
-                scores = jnp.where(allowed, s_ref[part, lanes], FILL)
-                highest = jnp.max(scores, axis=0, keepdims=True)
-                unscaled = jnp.exp2((scores - highest) * base2)
-                line = pl.ds(offset * subs + sub, 1)
-                chunk = p_ref[part, lanes]
+                scores = jnp.where(allowed, raw[part, lanes], FILL).reshape(size // 8, 8, LANES)
+                chunk = gradient[part, lanes]
+                highest = jnp.max(scores, axis=0)
+                unscaled = jnp.exp2((scores - highest[None]) * base2)
+                line = pl.ds((offset * subs + start // SUB) * 8, 8)
                 top[tile, line, lanes] = highest
-                total[tile, line, lanes] = jnp.sum(unscaled, axis=0, keepdims=True)
-                rowdot[tile, line, lanes] = jnp.sum(
-                    unscaled * chunk.astype(F32), axis=0, keepdims=True
-                )
-                probs[offset, tile, part, lanes] = unscaled.astype(BF16)
-                dprobs[offset, tile, part, lanes] = chunk
-
-    def forward(offset, keys, values, now, later):
-        tile, count, held = now
-        for lane in range(0, TILE, HALF):
-            if later is not None:
-                products(keys, values, later[1], later[0], lane, later[2])
-            softmax(offset, count, tile, lane, held)
-
-    even, unequal = (s_even, p_even), (s_odd, p_odd)
+                total[tile, line, lanes] = jnp.sum(unscaled, axis=0)
+                rowdot[tile, line, lanes] = jnp.sum(unscaled * chunk.reshape(scores.shape), axis=0)
+                probs[offset, tile, pl.ds(start, size), lanes] = unscaled.reshape(size, LANES).astype(BF16)
+                dprobs[offset, tile, pl.ds(start, size), lanes] = chunk.astype(BF16)
 
     def backward(offset, first, keys, key_count, tile):
         rows = rows_of(tile)
-        r = shift[tile].astype(BF16)
+        r = shift[tile]
         prob_parts = []
         score_parts = []
-        for sub in range(key_count // SUB):
-            part = pl.ds(sub * SUB, SUB)
-            w = weight[tile, pl.ds(offset * subs + sub, 1), :].astype(BF16)
-            prob_parts.append(probs[offset, tile, part, :] * w)
-            score_parts.append(prob_parts[-1] * (dprobs[offset, tile, part, :] - r))
+        for start, size in pieces(key_count):
+            part = pl.ds(start, size)
+            repeats = size // 16
+            w = weight[tile, pl.ds((offset * subs + start // SUB) * 16, 16), :]
+            prob_parts.append(probs[offset, tile, part, :] * jnp.concatenate([w] * repeats, axis=0))
+            score_parts.append(
+                prob_parts[-1] * (dprobs[offset, tile, part, :] - jnp.concatenate([r] * repeats, axis=0))
+            )
         prob = jnp.concatenate(prob_parts, axis=0)
         score = jnp.concatenate(score_parts, axis=0)
         dv_acc[pl.ds(0, key_count), :] += dot(prob, do_ref[rows, :], ((1,), (0,)))
@@ -211,29 +200,13 @@
 
     def over_own(body):
         for tile in range(tiles):
-            body(SUB * (((tile + 1) * toks + SUB - 1) // SUB), tile)
+            body(CUT * (((tile + 1) * toks + CUT - 1) // CUT), tile)
 
     def visit(offset):
-        keys, values = kbuf.at[offset - 1], vbuf.at[offset - 1]
-        ktrans[offset] = keys[...].T
-        for lane in range(0, TILE, HALF):
-            products(keys, values, block, 0, lane, even)
-
-        def step(pair, carry):
-            tile = 2 * pair
-            after = jnp.minimum(tile + 2, tiles - 1)
-            forward(offset, keys, values, (tile, block, even), (tile + 1, block, unequal))
-            forward(offset, keys, values, (tile + 1, block, unequal), (after, block, even))
-            return carry
-
-        lax.fori_loop(0, tiles // 2, step, 0)
-
-    own = []
-    over_own(lambda count, tile: own.append((tile, count, (even, unequal)[tile % 2])))
-    for lane in range(0, TILE, HALF):
-        products(k_ref, v_ref, own[0][1], 0, lane, even)
-    for now, later in zip(own, own[1:] + [None]):
-        forward(0, k_ref, v_ref, now, later)
+        ktrans[offset] = kbuf[offset - 1].T
+        over(functools.partial(forward, offset, kbuf.at[offset - 1], vbuf.at[offset - 1], block))
+
+    over_own(functools.partial(forward, 0, k_ref, v_ref))
     received(one)
 
     @pl.when(odd == 0)
@@ -255,8 +228,12 @@
         tops = top[tile]
         factors = jnp.exp2((tops - jnp.max(tops, axis=0, keepdims=True)) * base2)
         inverse = 1.0 / jnp.sum(factors * total[tile], axis=0, keepdims=True)
-        shift[tile] = jnp.sum(factors * rowdot[tile], axis=0, keepdims=True) * inverse
-        weight[tile] = factors * inverse
+        dotted = jnp.sum(factors * rowdot[tile], axis=0, keepdims=True) * inverse
+        shift[tile] = jnp.broadcast_to(dotted, (16, TILE)).astype(BF16)
+        scaled = factors * inverse
+        for group in range(SPAN * subs):
+            half = scaled[group * 8 : group * 8 + 8]
+            weight[tile, pl.ds(group * 16, 16), :] = jnp.concatenate([half, half], axis=0).astype(BF16)
 
     over(combine)
 
@@ -341,7 +318,7 @@
     scale = 1.0 / math.sqrt(width)
     doc = jnp.repeat(doc_start, heads).reshape(-1, 128)
     vmem = pl.BlockSpec(memory_space=pltpu.VMEM)
-    stat = (tiles, SPAN * (block // SUB), TILE)
+    stat = (tiles, SPAN * (block // SUB) * 8, TILE)
     results = pl.pallas_call(
         functools.partial(kernel, ctx_size, kv_size, block, heads, scale),
         out_shape=[
@@ -357,10 +334,6 @@
             pltpu.VMEM((block, width), BF16),
             pltpu.VMEM((rows, width), BF16),
             pltpu.VMEM((rows, width), BF16),
-            pltpu.VMEM((block, TILE), F32),
-            pltpu.VMEM((block, TILE), F32),
-            pltpu.VMEM((block, TILE), BF16),
-            pltpu.VMEM((block, TILE), BF16),
             pltpu.VMEM((SPAN - 1, block, width), BF16),
             pltpu.VMEM((SPAN - 1, block, width), BF16),
             pltpu.VMEM((kv_size,) + doc.shape, jnp.int32),
@@ -370,8 +343,8 @@
             pltpu.VMEM(stat, F32),
             pltpu.VMEM(stat, F32),
             pltpu.VMEM(stat, F32),
-            pltpu.VMEM(stat, F32),
-            pltpu.VMEM((tiles, 1, TILE), F32),
+            pltpu.VMEM((tiles, 2 * stat[1], TILE), BF16),
+            pltpu.VMEM((tiles, 16, TILE), BF16),
             pltpu.VMEM((SPAN, width, block), BF16),
             pltpu.VMEM((tiles, width, TILE), F32),
             pltpu.VMEM((block, width), F32),

time: 52.5 us -> 48.1 us (0.916)
  Pallas kernels: 50.2 us -> 45.8 us
    pallas_call x1, Pallas kernels: 48 us -> 43.6 us  [local(): pl.pallas_call(functools.partial(kernel, ctx_size, kv_size, block, heads,...]
where the time goes in v4:
time: 48.1 us; the launch traced here: 47.9 us
  Pallas kernels  45.8 us (95%)
  local copies, waits for them, and re-layouts  1.5 us (3%)
  between operations  0.65 us (1%)
    pallas_call x1, Pallas kernels, local(): pl.pallas_call(functools.partial(kernel, ctx_size, kv_size, block, heads,...  43.6 us
    pallas_call x1, Pallas kernels, local(): pl.pallas_call(hand_over, out_shape=[jax.ShapeDtypeStruct(x.shape, x.dtyp...  2.15 us

profile of v4, /device:TPU:3, one launch (start us, length us, event | category | flops | bytes accessed | tf_op | source)
XLA Modules:
  0.0 47.9 jit_solution(15133944360648398462)
XLA Ops:
  0.6 0.0 copy-start
  0.6 0.6 %copy-done = s32[128]{0:T(128)S(1)} copy-done((s32[128]{0:T(128)S(1)}, s32[128]{0:T(128)}, u32[]{:S(2)}) %copy-start) | copy-done | bytes 536
  1.3 0.1 broadcast_in_dim.7
  1.4 0.1 broadcast_in_dim.8
  1.4 0.7 %broadcast_in_dim.9.doc_any = s32[8,128]{1,0:T(8,128)} reshape(s32[8,16,8]{2,1,0:T(8,128)S(1)} %broadcast_in_dim.8) | data formatting | bytes 8192 | tf_op jit(solution)/shard_map/broadcast_in_dim | solution.py:319
  2.1 43.6 %attention_backward.1 = (bf16[4096,128]{1,0:T(8,128)(2,1)}, bf16[512,128]{1,0:T(8,128)(2,1)}, bf16[512,128]{1,0:T(8,128)(2,1)}) custom-call(bf16[4096,128]{1,0:T(8,128)(2,1)} %bitcast.7, bf16[512,128]{1,0:T(8,128)(2,1)} %bitcast.10, bf16[512,128]{1,0:T(8,128)(2,1)} %bitcast.11, bf16[4096,128]{1,0:T(8,128)(2,1)} %bitcast.8, s32[8,128]{1,0:T(8,128)} %broadcast_in_dim.9.doc_any), custom_call_target="tpu_custom_call" | custom-call | flops 10737418240 | bytes 4194304 | tf_op jit(solution)/shard_map/attention_backward/pallas_call | solution.py:322
  45.8 2.1 %hand_over.1 = (bf16[4096,128]{1,0:T(8,128)(2,1)}, bf16[512,128]{1,0:T(8,128)(2,1)}, bf16[512,128]{1,0:T(8,128)(2,1)}) custom-call(bf16[4096,128]{1,0:T(8,128)(2,1)} %get-tuple-element.9.dq_in, bf16[512,128]{1,0:T(8,128)(2,1)} %get-tuple-element.10.dk_in, bf16[512,128]{1,0:T(8,128)(2,1)} %get-tuple-element.11.dv_in), custom_call_target="tpu_custom_call" | custom-call | tf_op jit(solution)/shard_map/hand_over/pallas_call | solution.py:378
Async XLA Ops:
  0.6 0.7 %copy-start = (s32[128]{0:T(128)S(1)}, s32[128]{0:T(128)}, u32[]{:S(2)}) copy-start(s32[128]{0:T(128)} %param.9) | copy-start | bytes 1540

commit v5 on v4

--- a/solution.py
+++ b/solution.py
@@ -158,49 +158,52 @@
                 dprobs[offset, tile, pl.ds(start, size), lanes] = chunk.astype(BF16)
 
     def backward(offset, first, keys, key_count, tile):
-        rows = rows_of(tile)
-        r = shift[tile]
-        prob_parts = []
-        score_parts = []
-        for start, size in pieces(key_count):
-            part = pl.ds(start, size)
-            repeats = size // 16
-            w = weight[tile, pl.ds((offset * subs + start // SUB) * 16, 16), :]
-            prob_parts.append(probs[offset, tile, part, :] * jnp.concatenate([w] * repeats, axis=0))
-            score_parts.append(
-                prob_parts[-1] * (dprobs[offset, tile, part, :] - jnp.concatenate([r] * repeats, axis=0))
-            )
-        prob = jnp.concatenate(prob_parts, axis=0)
-        score = jnp.concatenate(score_parts, axis=0)
-        dv_acc[pl.ds(0, key_count), :] += dot(prob, do_ref[rows, :], ((1,), (0,)))
-        dk_acc[pl.ds(0, key_count), :] += dot(score, q_ref[rows, :], ((1,), (0,)))
-        part = dot(ktrans[offset, :, pl.ds(0, key_count)], score, ((1,), (0,)))
+        rows = pl.ds(pl.multiple_of(tile * TILE, 2 * TILE), 2 * TILE)
+        probs_of, scores_of = [], []
+        for now in (tile, tile + 1):
+            r = shift[now]
+            prob_parts, score_parts = [], []
+            for start, size in pieces(key_count):
+                part = pl.ds(start, size)
+                repeats = size // 16
+                w = weight[now, pl.ds((offset * subs + start // SUB) * 16, 16), :]
+                prob_parts.append(probs[offset, now, part, :] * jnp.concatenate([w] * repeats, axis=0))
+                score_parts.append(
+                    prob_parts[-1] * (dprobs[offset, now, part, :] - jnp.concatenate([r] * repeats, axis=0))
+                )
+            probs_of.append(jnp.concatenate(prob_parts, axis=0))
+            scores_of.append(jnp.concatenate(score_parts, axis=0))
+        score = jnp.concatenate(scores_of, axis=1)
+        count = pl.ds(0, key_count)
+        dv_acc[count, :] += dot(jnp.concatenate(probs_of, axis=1), do_ref[rows, :], ((1,), (0,)))
+        dk_acc[count, :] += dot(score, q_ref[rows, :], ((1,), (0,)))
+        part = dot(ktrans[offset, :, count], score, ((1,), (0,)))
+        pair = tile // 2
         if first:
-            dq_acc[tile] = part
+            dq_acc[pair] = part
         elif offset > 0:
-            dq_acc[tile] += part
+            dq_acc[pair] += part
         else:
-            dq_ref[rows, :] = ((dq_acc[tile] + part) * scale).T.astype(BF16)
-            stores[tile].start()
-
+            dq_ref[rows, :] = ((dq_acc[pair] + part) * scale).T.astype(BF16)
+            stores[pair].start()
+
+    pair_rows = [pl.ds(start, 2 * TILE) for start in range(0, tiles * TILE, 2 * TILE)]
     stores = [
-        pltpu.make_async_copy(
-            dq_ref.at[pl.ds(tile * TILE, TILE), :], dq_any.at[pl.ds(tile * TILE, TILE), :], store_sem.at[tile]
-        )
-        for tile in range(tiles)
+        pltpu.make_async_copy(dq_ref.at[part, :], dq_any.at[part, :], store_sem.at[pair])
+        for pair, part in enumerate(pair_rows)
     ]
 
-    def over(body):
-        def step(pair, carry):
-            body(2 * pair)
-            body(2 * pair + 1)
+    def over(body, stride=1):
+        def step(index, carry):
+            for part in range(0, 4, stride):
+                body(4 * index + part)
             return carry
 
-        lax.fori_loop(0, tiles // 2, step, 0)
-
-    def over_own(body):
-        for tile in range(tiles):
-            body(CUT * (((tile + 1) * toks + CUT - 1) // CUT), tile)
+        lax.fori_loop(0, tiles // 4, step, 0)
+
+    def over_own(body, stride=1):
+        for tile in range(0, tiles, stride):
+            body(CUT * (((tile + stride) * toks + CUT - 1) // CUT), tile)
 
     def visit(offset):
         ktrans[offset] = kbuf[offset - 1].T
@@ -240,7 +243,7 @@
     def accumulate(offset, first):
         dk_acc[...] = jnp.zeros_like(dk_acc)
         dv_acc[...] = jnp.zeros_like(dv_acc)
-        over(functools.partial(backward, offset, first, kbuf.at[offset - 1], block))
+        over(functools.partial(backward, offset, first, kbuf.at[offset - 1], block), 2)
         dk_acc[...] = dk_acc[...] * scale
 
     grad_sends, grad_recvs = (send_gk, send_gv), (recv_gk, recv_gv)
@@ -279,7 +282,7 @@
     given_one = give(1, ahead(-1))
     dk_acc[...] = jnp.zeros_like(dk_acc)
     dv_acc[...] = jnp.zeros_like(dv_acc)
-    over_own(functools.partial(backward, 0, False, k_ref))
+    over_own(functools.partial(backward, 0, False, k_ref), 2)
     dk_acc[...] = dk_acc[...] * scale
     received(given_three)
     take(2)
@@ -346,7 +349,7 @@
             pltpu.VMEM((tiles, 2 * stat[1], TILE), BF16),
             pltpu.VMEM((tiles, 16, TILE), BF16),
             pltpu.VMEM((SPAN, width, block), BF16),
-            pltpu.VMEM((tiles, width, TILE), F32),
+            pltpu.VMEM((tiles // 2, width, 2 * TILE), F32),
             pltpu.VMEM((block, width), F32),
             pltpu.VMEM((block, width), F32),
             pltpu.VMEM((SPAN - 1, block, width), BF16),
@@ -357,7 +360,7 @@
         + [pltpu.SemaphoreType.DMA((SPAN - 1,))] * 4
         + [pltpu.SemaphoreType.DMA((kv_size - 1,))] * 2
         + [pltpu.SemaphoreType.DMA((SPAN - 1,))] * 4
-        + [pltpu.SemaphoreType.DMA((5,)), pltpu.SemaphoreType.DMA((tiles,))],
+        + [pltpu.SemaphoreType.DMA((5,)), pltpu.SemaphoreType.DMA((tiles // 2,))],
         compiler_params=pltpu.CompilerParams(
             collective_id=0, has_side_effects=True, vmem_limit_bytes=56 * 1024 * 1024
         ),

time: 48.1 us -> 47.6 us (0.990)
  Pallas kernels: 45.8 us -> 45.1 us
    pallas_call x1, Pallas kernels: 43.6 us -> 43 us  [local(): pl.pallas_call(functools.partial(kernel, ctx_size, kv_size, block, heads,...]
where the time goes in v5:
time: 47.6 us; the launch traced here: 47.4 us
  Pallas kernels  45.1 us (95%)
  local copies, waits for them, and re-layouts  1.5 us (3%)
  between operations  0.81 us (2%)
    pallas_call x1, Pallas kernels, local(): pl.pallas_call(functools.partial(kernel, ctx_size, kv_size, block, heads,...  43 us
    pallas_call x1, Pallas kernels, local(): pl.pallas_call(hand_over, out_shape=[jax.ShapeDtypeStruct(x.shape, x.dtyp...  2.15 us

profile of v5, /device:TPU:3, one launch (start us, length us, event | category | flops | bytes accessed | tf_op | source)
XLA Modules:
  0.0 47.4 jit_solution(1519600116467270030)
XLA Ops:
  0.6 0.0 copy-start
  0.6 0.6 %copy-done = s32[128]{0:T(128)S(1)} copy-done((s32[128]{0:T(128)S(1)}, s32[128]{0:T(128)}, u32[]{:S(2)}) %copy-start) | copy-done | bytes 536
  1.3 0.1 broadcast_in_dim.7
  1.4 0.1 broadcast_in_dim.8
  1.4 0.7 %broadcast_in_dim.9.doc_any = s32[8,128]{1,0:T(8,128)} reshape(s32[8,16,8]{2,1,0:T(8,128)S(1)} %broadcast_in_dim.8) | data formatting | bytes 8192 | tf_op jit(solution)/shard_map/broadcast_in_dim | solution.py:322
  2.1 43.0 %attention_backward.1 = (bf16[4096,128]{1,0:T(8,128)(2,1)}, bf16[512,128]{1,0:T(8,128)(2,1)}, bf16[512,128]{1,0:T(8,128)(2,1)}) custom-call(bf16[4096,128]{1,0:T(8,128)(2,1)} %bitcast.7, bf16[512,128]{1,0:T(8,128)(2,1)} %bitcast.10, bf16[512,128]{1,0:T(8,128)(2,1)} %bitcast.11, bf16[4096,128]{1,0:T(8,128)(2,1)} %bitcast.8, s32[8,128]{1,0:T(8,128)} %broadcast_in_dim.9.doc_any), custom_call_target="tpu_custom_call" | custom-call | flops 10737418240 | bytes 4194304 | tf_op jit(solution)/shard_map/attention_backward/pallas_call | solution.py:325
  45.1 2.1 %hand_over.1 = (bf16[4096,128]{1,0:T(8,128)(2,1)}, bf16[512,128]{1,0:T(8,128)(2,1)}, bf16[512,128]{1,0:T(8,128)(2,1)}) custom-call(bf16[4096,128]{1,0:T(8,128)(2,1)} %get-tuple-element.9.dq_in, bf16[512,128]{1,0:T(8,128)(2,1)} %get-tuple-element.10.dk_in, bf16[512,128]{1,0:T(8,128)(2,1)} %get-tuple-element.11.dv_in), custom_call_target="tpu_custom_call" | custom-call | tf_op jit(solution)/shard_map/hand_over/pallas_call | solution.py:381
Async XLA Ops:
  0.6 0.7 %copy-start = (s32[128]{0:T(128)S(1)}, s32[128]{0:T(128)}, u32[]{:S(2)}) copy-start(s32[128]{0:T(128)} %param.9) | copy-start | bytes 1540
